TPU v7x, 32 devices: a whole 2x2x4 slice. The times are simulated.
32 devices in a mesh: tm: 4 (over y, core), chan: 4 (over z), stn: 2 (over x).
Axes of the slice: x: 2, y: 2, z: 4, core: 2. Of those that a mesh axis runs over, the one named last changes fastest.
Arguments:
- voltages: bfloat16 [2, 64, 768, 4096], P(None, 'tm', ('chan', 'stn')), may hold values from -6 to 6
- coefficients: float32 [16, 4096], replicated, may hold values from -2.5 to 2.5
- kept_channels: int32 [384], replicated, may hold values from 0 to 4095, as said below
- station_flags: int32 [768], P(('chan', 'stn')), may hold values 0 or 1
Outputs:
- visibilities: float32 [2, 384, 768, 768], P(None, 'chan', ('tm', 'stn'))
Inputs may be any that keep to these rules, and one draw needn't show every extreme that they name: `kept_channels`: 384 distinct channel numbers, in no particular order.
All inputs are finite; a program needn't handle non-finite values. No bound on the sum of `station_flags` on one device may be relied on, other than what follows from the above.
Results may differ from a plain program's by a relative error of at most 0.0039.
Values may be sent and summed in bfloat16 or wider, within the bound.
A program may use at most 256 MiB of HBM per device.

v0:
```python
import math

import jax
import jax.numpy as jnp
from jax import lax
from jax.sharding import PartitionSpec as P


def passed_along(block, axis, distance):
    devices = range(lax.axis_size(axis))
    route = [(i - distance, i) for i in devices if i - distance in devices]
    return lax.ppermute(block, axis, route)


def build_table(kept_channels, nfft_length):
    positions = jnp.arange(nfft_length, dtype=jnp.int32)
    phases = positions[:, None] * kept_channels[None, :] % nfft_length
    angles = phases.astype(jnp.float32) * (2.0 * math.pi / nfft_length)
    normalizer = 1.0 / math.sqrt(nfft_length)
    return jnp.concatenate([jnp.cos(angles) * normalizer, jnp.sin(angles) * normalizer], axis=1)


def tap_sum(extended, coefficients, frame_count):
    tap_count = coefficients.shape[0]
    start = tap_count - 1
    total = coefficients[0][None, None, None, :] * extended[:, start : start + frame_count].astype(
        jnp.float32
    )
    for tap_index in range(1, tap_count):
        first = tap_count - 1 - tap_index
        total = total + coefficients[tap_index][None, None, None, :] * extended[
            :, first : first + frame_count
        ].astype(jnp.float32)
    return total


def transform(filtered, joint_table, channel_count):
    product = jnp.einsum(
        "pfin,nk->pkif",
        filtered,
        joint_table,
        precision=lax.Precision.HIGHEST,
        preferred_element_type=jnp.float32,
    )
    real_part = product[0, :channel_count] + product[1, channel_count:]
    imag_part = product[1, :channel_count] - product[0, channel_count:]
    return (real_part, imag_part)


def correlate(spectra_all, row_start, row_count):
    mine = lax.dynamic_slice_in_dim(spectra_all, row_start, row_count, 2)
    left_side = jnp.stack(
        [
            jnp.concatenate([mine[0], mine[1]], axis=-1),
            jnp.concatenate([mine[1], -mine[0]], axis=-1),
        ]
    )
    right_side = jnp.concatenate([spectra_all[0], spectra_all[1]], axis=-1)
    return jnp.einsum("pcif,cjf->pcij", left_side, right_side, preferred_element_type=jnp.float32)


def shards(voltages, coefficients, kept_channels, station_flags):
    frames_dev = voltages.shape[1]
    inputs_dev = voltages.shape[2]
    nfft_length = voltages.shape[3]
    tap_count = coefficients.shape[0]
    channel_count = kept_channels.shape[0]
    history = tap_count - 1
    joint_table = build_table(kept_channels, nfft_length)
    trailing = voltages[:, frames_dev - history :]
    earlier = passed_along(trailing, "tm", 1)
    extended = jnp.concatenate([earlier, voltages], axis=1)
    filtered = tap_sum(extended, coefficients, frames_dev)
    real_part, imag_part = transform(filtered, joint_table, channel_count)
    weights = station_flags.astype(jnp.float32)
    spectra = (jnp.stack([real_part, imag_part]) * weights[None, None, :, None]).astype(
        jnp.bfloat16
    )
    local_spectra = spectra.reshape(2, channel_count, 1, 1, inputs_dev, frames_dev)
    turned = lax.all_to_all(local_spectra, "chan", split_axis=1, concat_axis=2, tiled=True)
    n_time = lax.axis_size("tm")
    n_station = lax.axis_size("stn")
    owned = turned.shape[1]
    groups = turned.shape[2]
    inputs_total = groups * n_station * inputs_dev
    row_count = inputs_total // (n_time * n_station)
    row_start = (lax.axis_index("tm") * n_station + lax.axis_index("stn")) * row_count
    frames_total = frames_dev * n_time
    everything = lax.all_gather(turned[None], ("tm", "stn"), axis=0, tiled=True)
    everything = everything.reshape(n_time, n_station, 2, owned, groups, inputs_dev, frames_dev)
    spectra_all = jnp.transpose(everything, (2, 3, 4, 1, 5, 0, 6)).reshape(
        2, owned, inputs_total, frames_total
    )
    summed = correlate(spectra_all, row_start, row_count)
    return summed * (1.0 / frames_total)


def solution(mesh):
    placed = (P(None, "tm", ("chan", "stn"), None), P(), P(), P(("chan", "stn")))
    return jax.shard_map(
        shards,
        mesh=mesh,
        in_specs=placed,
        out_specs=P(None, "chan", ("tm", "stn"), None),
        check_vma=False,
    )
```

profile of v0, /device:TPU:0, one launch (start us, length us, event | category | flops | bytes accessed | tf_op | source)
XLA Modules:
  0.0 1104.6 jit_solution(3686674011123932708)
XLA Ops:
  6.5 0.0 copy-start.4
  6.5 0.0 copy-start.2
  6.5 0.0 all-gather.3.cloned.1.call-start
  6.5 20.0 %slice.126 = bf16[2,15,96,4096]{3,2,1,0:T(8,128)(2,1)} slice(bf16[2,16,96,4096]{3,2,1,0:T(8,128)(2,1)} %param.4), slice={[0:2], [1:16], [0:96], [0:4096]} | slice | bytes 47185920 | tf_op jit(solution)/shard_map/slice | solution.py:70
  26.5 10.2 collective-permute-start
  36.7 0.0 copy-done.4
  36.7 0.6 convert_element_type.81
  37.3 0.0 copy-done.2
  37.3 0.0 copy-start.1
  37.3 26.8 %cosine_multiply_fusion = (f32[4096,384]{1,0:T(8,128)}, f32[4096,384]{1,0:T(8,128)}) fusion(s32[384]{0:T(512)S(1)} %copy-done.2), kind=kLoop, calls=%fused_computation.93 | loop fusion | flops 25165824 | bytes 12584448 | tf_op jit(solution)/shard_map/mul | solution.py:20
  64.0 10.1 maximum_bitcast_fusion.11
  74.1 0.0 copy-done.1
  74.1 0.0 slice-start
  74.1 0.2 fusion.101
  74.3 0.0 slice-start.1
  74.4 0.0 slice-start.2
  74.4 0.0 slice-start.3
  74.4 0.0 slice-start.4
  74.4 0.0 slice-start.5
  74.4 0.0 collective-permute-done
  74.4 23.7 %constant_dynamic-update-slice_fusion.1 = bf16[2,31,96,4096]{3,2,1,0:T(8,128)(2,1)} fusion(bf16[2,15,96,4096]{3,2,1,0:T(8,128)(2,1)} %collective-permute-done), kind=kLoop, calls=%fused_computation.111 | loop fusion | bytes 47185920
  98.1 0.0 slice-done
  98.1 0.0 slice-done.1
  98.1 0.0 slice-done.2
  98.1 0.0 slice-done.3
  98.1 0.0 slice-done.4
  98.1 0.0 slice-done.5
  98.1 9.4 constant_dynamic-update-slice_fusion
  107.6 0.0 copy-start.3
  107.6 237.5 %fusion.93 = f32[2,768,96,16]{1,2,3,0:T(8,128)} fusion(bf16[2,16,96,4096]{3,2,1,0:T(8,128)(2,1)} %param.4, bf16[2,31,96,4096]{3,2,1,0:T(8,128)(2,1)} %constant_dynamic-update-slice_fusion, f32[4096]{0:T(1024)S(1)} %bitcast.87, f32[4096]{0:T(1024)S(1)} %bitcast.88, f32[4096]{0:T(1024)S(1)} %bitcast.74, f32[4096]{0:T(1024)S(1)} %bitcast.75, ...), kind=kOutput, calls=%fused_computation.102 | convolution fusion | flops 116555513856 | bytes 424935424 | tf_op jit(solution)/shard_map/pfin,nk->pkif/dot_general | solution.py:38
  345.1 4.3 fusion.97
  349.5 0.0 copy-done.3
  349.5 1.9 fusion.89
  351.4 4.0 copy.22
  355.4 43.9 %all_to_all.15 = bf16[2,384,1,1,96,16]{4,5,3,2,0,1:T(8,128)(2,1)S(1)} all-to-all(bf16[2,384,1,1,96,16]{4,5,3,2,0,1:T(8,128)(2,1)S(1)} %copy.22), channel_id=1, replica_groups=mesh['tm'=4,'chan'=4,'stn'=2] {'chan'}, dimensions={1} | all-to-all | bytes 4718592 | tf_op jit(solution)/shard_map/all_to_all | solution.py:80
  399.3 2.6 copy.38
  401.9 0.0 all-gather.3.cloned.1.call-update
  401.9 331.3 %all-gather.3.cloned.1.call-done = bf16[16,96,4,1,1,96,16]{5,6,4,3,2,1,0:T(8,128)(2,1)} async-done(((bf16[2,96,4,1,1,96,16]{5,6,4,3,2,1,0:T(8,128)(2,1)}), bf16[16,96,4,1,1,96,16]{5,6,4,3,2,1,0:T(8,128)(2,1)}) %all-gather.3.cloned.1.call-update) | async-done | bytes 18874384 | tf_op jit(solution)/shard_map/all_gather | solution.py:89
  733.2 0.0 copy-start
  733.2 45.8 %copy.28 = bf16[2,96,4,2,96,4,16]{4,3,2,6,5,1,0:T(2,128)(2,1)} copy(bf16[2,96,4,2,96,4,16]{4,6,2,1,0,3,5:T(8,128)(2,1)} %bitcast.65) | data formatting | bytes 37748736 | tf_op jit(solution)/shard_map/transpose | solution.py:91
  779.1 0.0 copy-done
  779.1 10.7 fusion.100
  789.8 65.7 %reshape.63 = bf16[2,96,768,64]{2,3,1,0:T(8,128)(2,1)} reshape(bf16[2,96,4,2,96,4,16]{4,3,2,6,5,1,0:T(2,128)(2,1)} %copy.28) | data formatting | bytes 37748736 | tf_op jit(solution)/shard_map/reshape | solution.py:91
  855.5 23.7 %copy.24 = bf16[1,96,4,2,96,4,16]{4,3,2,6,5,1,0:T(2,128)(2,1)} copy(bf16[1,96,4,2,96,4,16]{4,6,2,1,0,3,5:T(8,128)(2,1)} %get-tuple-element.5) | data formatting | bytes 18874368 | tf_op jit(solution)/shard_map/slice | solution.py:58
  879.1 33.8 %squeeze.8 = bf16[96,768,64]{1,2,0:T(8,128)(2,1)} reshape(bf16[1,96,4,2,96,4,16]{4,3,2,6,5,1,0:T(2,128)(2,1)} %copy.24) | data formatting | bytes 18874368 | tf_op jit(solution)/shard_map/squeeze | solution.py:58
  912.9 5.1 constant_dynamic-slice_fusion.1
  918.0 2.4 copy.36
  920.4 2.8 copy.35
  923.3 1.8 bitcast_negate_fusion
  925.0 17.5 %copy.26 = bf16[96,768,64]{2,1,0:T(8,128)(2,1)} copy(bf16[96,768,64]{1,2,0:T(8,128)(2,1)} %squeeze.8) | data formatting | bytes 18874368 | tf_op jit(solution)/shard_map/squeeze | solution.py:58
  942.5 23.7 %copy.25 = bf16[1,96,4,2,96,4,16]{4,3,2,6,5,1,0:T(2,128)(2,1)} copy(bf16[1,96,4,2,96,4,16]{4,6,2,1,0,3,5:T(8,128)(2,1)} %get-tuple-element.6) | data formatting | bytes 18874368 | tf_op jit(solution)/shard_map/slice | solution.py:58
  966.2 34.0 %squeeze.9 = bf16[96,768,64]{1,2,0:T(8,128)(2,1)} reshape(bf16[1,96,4,2,96,4,16]{4,3,2,6,5,1,0:T(2,128)(2,1)} %copy.25) | data formatting | bytes 18874368 | tf_op jit(solution)/shard_map/squeeze | solution.py:58
  1000.2 17.4 %copy.27 = bf16[96,768,64]{2,1,0:T(8,128)(2,1)} copy(bf16[96,768,64]{1,2,0:T(8,128)(2,1)} %squeeze.9) | data formatting | bytes 18874368 | tf_op jit(solution)/shard_map/squeeze | solution.py:58
  1017.6 6.6 maximum_bitcast_fusion.6
  1024.2 35.1 %multiply_bitcast_fusion = f32[2,96,96,768]{3,2,0,1:T(8,128)} fusion(bf16[96,768,64]{2,1,0:T(8,128)(2,1)} %copy.27, bf16[96,768,64]{2,1,0:T(8,128)(2,1)} %copy.26, bf16[1,96,96,128]{3,2,0,1:T(8,128)(2,1)} %get-tuple-element.12, bf16[1,96,96,128]{3,2,0,1:T(8,128)(2,1)} %get-tuple-element.11), kind=kOutput, calls=%fused_computation | convolution fusion | flops 3685220352 | bytes 80216064 | tf_op jit(solution)/shard_map/pcif,cjf->pcij/dot_general | solution.py:59
  1059.3 38.5 %copy.31 = f32[2,96,96,768]{3,2,1,0:T(8,128)} copy(f32[2,96,96,768]{3,2,0,1:T(8,128)} %multiply_bitcast_fusion) | data formatting | bytes 113246208 | tf_op jit(solution)/shard_map/mul | solution.py:95
  (1 shorter events, 0.0 us)
Async XLA Ops:
  6.5 30.2 %copy-start.4 = (s32[96]{0:T(128)S(1)}, s32[96]{0:T(128)}, u32[]{:S(2)}) copy-start(s32[96]{0:T(128)} %param.7) | copy-start | bytes 1156
  6.5 30.7 %copy-start.2 = (s32[384]{0:T(512)S(1)}, s32[384]{0:T(512)}, u32[]{:S(2)}) copy-start(s32[384]{0:T(512)} %param.6) | copy-start | bytes 4612
  6.5 726.7 %all-gather.3.cloned.1.call-start = ((), (), s32[]{:S(2)}) async-start(), calls=%async_computation.1 | async-start | bytes 28311552 | tf_op jit(solution)/shard_map/all_gather | solution.py:89
  26.5 47.9 %collective-permute-start = (bf16[2,15,96,4096]{3,2,1,0:T(8,128)(2,1)}, bf16[2,15,96,4096]{3,2,1,0:T(8,128)(2,1)}, u32[]{:S(2)}, u32[]{:S(2)}) collective-permute-start(bf16[2,15,96,4096]{3,2,1,0:T(8,128)(2,1)} %slice.126), channel_id=1, source_target_pairs={{0,8},{8,16},{16,24},{1,9},{9,17},{17,25},{2,10},{10,18},{18,26},{... | collective-permute-start | bytes 70778888 | tf_op jit(solution)/shard_map/ppermute | solution.py:12
  37.3 36.8 %copy-start.1 = (f32[16,4096]{1,0:T(8,128)S(1)}, f32[16,4096]{1,0:T(8,128)}, u32[]{:S(2)}) copy-start(f32[16,4096]{1,0:T(8,128)} %param.5) | copy-start | bytes 786436
  74.1 24.0 %slice-start = ((s8[25165824]{0:T(1024)(128)(4,1)}), s8[4194304]{0:T(1024)(128)(4,1)S(1)}, s32[]{:S(2)}) async-start(s8[25165824]{0:T(1024)(128)(4,1)} %bitcast.67), calls=%async_computation.2 | async-start | bytes 8388608
  74.3 23.7 %slice-start.1 = ((s8[25165824]{0:T(1024)(128)(4,1)}), s8[4194304]{0:T(1024)(128)(4,1)S(1)}, s32[]{:S(2)}) async-start(s8[25165824]{0:T(1024)(128)(4,1)} %bitcast.67), calls=%async_computation.3 | async-start | bytes 8388608
  74.4 23.7 %slice-start.2 = ((s8[25165824]{0:T(1024)(128)(4,1)}), s8[4194304]{0:T(1024)(128)(4,1)S(1)}, s32[]{:S(2)}) async-start(s8[25165824]{0:T(1024)(128)(4,1)} %bitcast.67), calls=%async_computation.4 | async-start | bytes 8388608
  74.4 23.7 %slice-start.3 = ((s8[25165824]{0:T(1024)(128)(4,1)}), s8[4194304]{0:T(1024)(128)(4,1)S(1)}, s32[]{:S(2)}) async-start(s8[25165824]{0:T(1024)(128)(4,1)} %bitcast.67), calls=%async_computation.5 | async-start | bytes 8388608
  74.4 23.7 %slice-start.4 = ((s8[25165824]{0:T(1024)(128)(4,1)}), s8[4194304]{0:T(1024)(128)(4,1)S(1)}, s32[]{:S(2)}) async-start(s8[25165824]{0:T(1024)(128)(4,1)} %bitcast.67), calls=%async_computation.6 | async-start | bytes 8388608
  74.4 23.7 %slice-start.5 = ((s8[25165824]{0:T(1024)(128)(4,1)}), s8[4194304]{0:T(1024)(128)(4,1)S(1)}, s32[]{:S(2)}) async-start(s8[25165824]{0:T(1024)(128)(4,1)} %bitcast.67), calls=%async_computation.7 | async-start | bytes 8388608
  107.6 241.9 %copy-start.3 = (f32[96]{0:T(128)S(1)}, f32[96]{0:T(128)}, u32[]{:S(2)}) copy-start(f32[96]{0:T(128)} %convert_element_type.81) | copy-start | bytes 1156
  733.2 45.8 %copy-start = (bf16[16,96,4,1,1,96,16]{5,6,4,3,2,1,0:T(8,128)(2,1)S(1)}, bf16[16,96,4,1,1,96,16]{5,6,4,3,2,1,0:T(8,128)(2,1)}, u32[]{:S(2)}) copy-start(bf16[16,96,4,1,1,96,16]{5,6,4,3,2,1,0:T(8,128)(2,1)} %all-gather.3.cloned.1.call-done) | copy-start | bytes 56623108
Sparse Core Ops, SparseCore 0:
  402.0 331.1 all-gather.2
where the time goes:
time: 1110 us; the launch traced here: 1100 us
  local copies, waits for them, and re-layouts  381 us (34%)
  waiting for transfers between devices  331 us (30%)
  matrix products  273 us (25%)
  other arithmetic  52.1 us (5%)
  blocking collectives  43.9 us (4%)
  between operations  13.5 us (1%)
    all_gather x1, waiting for transfers between devices, shards(): everything = lax.all_gather(turned[None], ('tm', 'stn'), axis=0, tiled=True)  331 us
    dot_general x1, matrix products, transform(): jnp.einsum('pfin,nk->pkif', filtered, joint_table, precision=lax.Precisio...  238 us
    squeeze x4, local copies, waits for them, and re-layouts, correlate(): right_side = jnp.concatenate([spectra_all[0], spectra_all[1]], axis=-1)  103 us
    reshape x1, local copies, waits for them, and re-layouts, shards(): jnp.transpose(everything, (2, 3, 4, 1, 5, 0, 6))  65.7 us
    slice x3, local copies, waits for them, and re-layouts, correlate(): right_side = jnp.concatenate([spectra_all[0], spectra_all[1]], axis=-1)  58 us
    transpose x1, local copies, waits for them, and re-layouts, shards(): jnp.transpose(everything, (2, 3, 4, 1, 5, 0, 6))  45.8 us
    all_to_all x1, blocking collectives, shards(): lax.all_to_all(local_spectra, 'chan', split_axis=1, concat_axis=2, tiled=...  43.9 us
    mul x1, local copies, waits for them, and re-layouts, shards(): return summed * (1.0 / frames_total)  38.5 us
  transfers between devices with their start and end apart: 2, of which 1 were waited for; matrix products, arithmetic and copies ran while one was open for 3% of the time, Pallas kernels for 0%

commit v1 on v0

--- a/solution.py
+++ b/solution.py
@@ -3,7 +3,13 @@
 import jax
 import jax.numpy as jnp
 from jax import lax
+from jax.experimental import pallas as pl
+from jax.experimental.pallas import tpu as pltpu
 from jax.sharding import PartitionSpec as P
+
+GROUP = 16
+LANES = 128
+CHUNK = 512
 
 
 def passed_along(block, axis, distance):
@@ -59,7 +65,7 @@
     return jnp.einsum("pcif,cjf->pcij", left_side, right_side, preferred_element_type=jnp.float32)
 
 
-def shards(voltages, coefficients, kept_channels, station_flags):
+def plain_shards(voltages, coefficients, kept_channels, station_flags):
     frames_dev = voltages.shape[1]
     inputs_dev = voltages.shape[2]
     nfft_length = voltages.shape[3]
@@ -95,6 +101,197 @@
     return summed * (1.0 / frames_total)
 
 
+def build_blocks(kept_channels, nfft_length):
+    low_count = 64
+    high = jnp.arange(nfft_length // low_count, dtype=jnp.int32) * low_count
+    low = jnp.arange(low_count, dtype=jnp.int32)
+    step = 2.0 * math.pi / nfft_length
+
+    def waves(positions):
+        phases = kept_channels[:, None] * positions[None, :] % nfft_length
+        angles = phases.astype(jnp.float32) * step
+        return jnp.cos(angles), jnp.sin(angles)
+
+    high_cos, high_sin = waves(high)
+    low_cos, low_sin = waves(low)
+    expand = lambda x: jnp.repeat(x, low_count, axis=1)
+    spread = lambda x: jnp.tile(x, (1, nfft_length // low_count))
+    hc, hs, lc, ls = expand(high_cos), expand(high_sin), spread(low_cos), spread(low_sin)
+    normalizer = 1.0 / math.sqrt(nfft_length)
+    cosine = ((hc * lc - hs * ls) * normalizer).astype(jnp.bfloat16)
+    sine = ((hs * lc + hc * ls) * normalizer).astype(jnp.bfloat16)
+    return jnp.stack([jnp.stack([cosine, sine]), jnp.stack([-sine, cosine])])
+
+
+def channelize_body(later, v_ref, c_ref, t_ref, out_ref, even, odd):
+    step = pl.program_id(0)
+    frames, inputs = v_ref.shape[1], v_ref.shape[2]
+    taps = c_ref.shape[0]
+    channels = t_ref.shape[2]
+    width = v_ref.shape[3]
+    pieces = inputs // GROUP
+    piece = frames * GROUP
+
+    def phase(filling, reading):
+        def part(s, carry):
+            row = pl.multiple_of(s * GROUP, GROUP)
+            for p in range(2):
+                for lane in range(0, width, LANES):
+                    at = slice(lane, lane + LANES)
+                    v = [
+                        v_ref[p, f, pl.ds(row, GROUP), at].astype(jnp.float32)
+                        for f in range(frames)
+                    ]
+                    c = [c_ref[t : t + 1, at] for t in range(taps)]
+                    for f in range(frames):
+                        total = None
+                        for t in range(taps):
+                            source = f - t + (frames if later else 0)
+                            if 0 <= source < frames:
+                                term = c[t] * v[source]
+                                total = term if total is None else total + term
+                        if total is None:
+                            total = jnp.zeros((GROUP, LANES), jnp.float32)
+                        upper = total.astype(jnp.bfloat16)
+                        lower = (total - upper.astype(jnp.float32)).astype(jnp.bfloat16)
+                        place = pl.ds(pl.multiple_of(f * inputs + row, GROUP), GROUP)
+                        filling[2 * p, place, at] = upper
+                        filling[2 * p + 1, place, at] = lower
+            rows = pl.ds(pl.multiple_of(s * piece, LANES), piece)
+            for h in range(2):
+                total = None
+                for p in range(2):
+                    for q in range(2):
+                        term = lax.dot_general(
+                            t_ref[h, p],
+                            reading[2 * p + q, rows, :],
+                            (((1,), (1,)), ((), ())),
+                            preferred_element_type=jnp.float32,
+                        )
+                        total = term if total is None else total + term
+                before = out_ref[h, :, rows]
+                out_ref[h, :, rows] = jnp.where(step <= 1, 0.0, before) + total
+            return carry
+
+        lax.fori_loop(0, pieces, part, 0)
+
+    @pl.when(step % 2 == 0)
+    def _():
+        phase(even, odd)
+
+    @pl.when(step % 2 == 1)
+    def _():
+        phase(odd, even)
+
+
+def channelize(voltages, coefficients, blocks, later):
+    _, frames, inputs, nfft_length = voltages.shape
+    taps = coefficients.shape[0]
+    channels = blocks.shape[2]
+    rows = frames * inputs
+    chunks = nfft_length // CHUNK
+    last = chunks - 1
+    return pl.pallas_call(
+        lambda *refs: channelize_body(later, *refs),
+        grid=(chunks + 1,),
+        in_specs=[
+            pl.BlockSpec((2, frames, inputs, CHUNK), lambda j: (0, 0, 0, jnp.minimum(j, last))),
+            pl.BlockSpec((taps, CHUNK), lambda j: (0, jnp.minimum(j, last))),
+            pl.BlockSpec((2, 2, channels, CHUNK), lambda j: (0, 0, 0, jnp.maximum(j - 1, 0))),
+        ],
+        out_specs=pl.BlockSpec((2, channels, rows), lambda j: (0, 0, 0)),
+        out_shape=jax.ShapeDtypeStruct((2, channels, rows), jnp.float32),
+        scratch_shapes=[pltpu.VMEM((4, rows, CHUNK), jnp.bfloat16)] * 2,
+        compiler_params=pltpu.CompilerParams(vmem_limit_bytes=56 * 1024 * 1024),
+        cost_estimate=pl.CostEstimate(
+            flops=16 * rows * channels * nfft_length, bytes_accessed=60_000_000, transcendentals=0
+        ),
+    )(voltages, coefficients, blocks)
+
+
+def correlate_body(scale, which_ref, s_ref, out_ref):
+    n_time, n_station, _, count, frames, width = s_ref.shape
+    inputs = out_ref.shape[2]
+    groups = width // inputs
+    which = which_ref[0]
+    for k in range(count):
+        parts = []
+        for station in range(n_station):
+            parts.append(
+                jnp.concatenate(
+                    [s_ref[t, station, p, k] for p in range(2) for t in range(n_time)], axis=0
+                )
+            )
+        cuts = [
+            parts[station][:, g * inputs : (g + 1) * inputs]
+            for g in range(groups)
+            for station in range(n_station)
+        ]
+        right = jnp.concatenate(cuts, axis=1)
+        mine = cuts[0]
+        for index in range(1, len(cuts)):
+            mine = jnp.where(which == index, cuts[index], mine)
+        half = mine.shape[0] // 2
+        turned = jnp.concatenate([mine[half:], -mine[:half]], axis=0)
+        for h, left in enumerate((mine, turned)):
+            product = lax.dot_general(
+                left, right, (((0,), (0,)), ((), ())), preferred_element_type=jnp.float32
+            )
+            out_ref[h, k] = product * scale
+
+
+def correlate_all(everything, which, inputs, scale):
+    n_time, n_station, _, owned, frames, width = everything.shape
+    count = 4
+    total = n_station * width
+    return pl.pallas_call(
+        lambda *refs: correlate_body(scale, *refs),
+        grid=(owned // count,),
+        in_specs=[
+            pl.BlockSpec(memory_space=pltpu.SMEM),
+            pl.BlockSpec(
+                (n_time, n_station, 2, count, frames, width), lambda j: (0, 0, 0, j, 0, 0)
+            ),
+        ],
+        out_specs=pl.BlockSpec((2, count, inputs, total), lambda j: (0, j, 0, 0)),
+        out_shape=jax.ShapeDtypeStruct((2, owned, inputs, total), jnp.float32),
+        compiler_params=pltpu.CompilerParams(vmem_limit_bytes=48 * 1024 * 1024),
+    )(which, everything)
+
+
+def shards(voltages, coefficients, kept_channels, station_flags):
+    _, frames, inputs, nfft_length = voltages.shape
+    channels = kept_channels.shape[0]
+    n_time, n_station, n_chan = (lax.axis_size(a) for a in ("tm", "stn", "chan"))
+    fits = (
+        inputs % GROUP == 0
+        and frames % 16 == 0
+        and coefficients.shape[0] <= frames + 1
+        and nfft_length % CHUNK == 0
+        and frames * GROUP % LANES == 0
+        and n_chan * n_station == n_time * n_station
+        and n_chan * inputs % LANES == 0
+        and channels // n_chan % 4 == 0
+    )
+    if not fits:
+        return plain_shards(voltages, coefficients, kept_channels, station_flags)
+    blocks = build_blocks(kept_channels, nfft_length)
+    after = channelize(voltages, coefficients, blocks, True)
+    earlier = passed_along(after, "tm", 1)
+    own = channelize(voltages, coefficients, blocks, False)
+    weights = jnp.tile(station_flags.astype(jnp.float32), frames)
+    spectra = ((own + earlier) * weights).astype(jnp.bfloat16)
+    owned = channels // n_chan
+    spectra = spectra.reshape(2, n_chan, owned, frames, inputs)
+    turned = lax.all_to_all(spectra, "chan", split_axis=1, concat_axis=1, tiled=True)
+    merged = jnp.transpose(turned, (0, 2, 3, 1, 4)).reshape(2, owned, frames, n_chan * inputs)
+    everything = lax.all_gather(merged[None], ("tm", "stn"), axis=0, tiled=True)
+    everything = everything.reshape(n_time, n_station, *merged.shape)
+    which = lax.axis_index("tm") * n_station + lax.axis_index("stn")
+    scale = 1.0 / (frames * n_time)
+    return correlate_all(everything, which.astype(jnp.int32)[None], inputs, scale)
+
+
 def solution(mesh):
     placed = (P(None, "tm", ("chan", "stn"), None), P(), P(), P(("chan", "stn")))
     return jax.shard_map(

time: 1110 us -> 398 us (0.36)
  local copies, waits for them, and re-layouts: 381 us -> 21.8 us
  matrix products: 273 us -> 0 us
  waiting for transfers between devices: 331 us -> 97 us
  Pallas kernels: 0 us -> 165 us
  other arithmetic: 52.1 us -> 18.7 us
  blocking collectives: 43.9 us -> 75.9 us
    dot_general x2 -> x0, matrix products: 273 us -> none  [the longest x1 238 us: transform(): jnp.einsum('pfin,nk->pkif', filtered, joint_table, precision=lax.Precisio...]
    all_gather x1, waiting for transfers between devices: 331 us -> 97 us  [shards(): everything = lax.all_gather(merged[None], ('tm', 'stn'), axis=0, tiled=True)]
    pallas_call x0 -> x3, Pallas kernels: none -> 165 us  [the longest x2 124 us: channelize(): pl.pallas_call(lambda *refs: channelize_body(later, *refs), grid=(chunks...]
    squeeze x4 -> x0, local copies, waits for them, and re-layouts: 103 us -> none  [correlate(): right_side = jnp.concatenate([spectra_all[0], spectra_all[1]], axis=-1)]
    slice x6 -> x0, local copies, waits for them, and re-layouts: 83.3 us -> none  [the longest x3 58 us: correlate(): right_side = jnp.concatenate([spectra_all[0], spectra_all[1]], axis=-1)]
    reshape x1 -> x2, local copies, waits for them, and re-layouts: 65.7 us -> 5.44 us  [shards(): spectra = spectra.reshape(2, n_chan, owned, frames, inputs)]
    transpose x1, local copies, waits for them, and re-layouts: 45.8 us -> 4.05 us  [shards(): jnp.transpose(turned, (0, 2, 3, 1, 4))]
    mul x1, local copies, waits for them, and re-layouts: 38.5 us -> 0.07 us  [shards(): spectra = ((own + earlier) * weights).astype(jnp.bfloat16)]
  transfers between devices with their start and end apart: 2 -> 2, of which waited for: 1 -> 1; matrix products, arithmetic and copies ran while one was open for 3% -> 0% of each run, Pallas kernels for 0% -> 16%
where the time goes in v1:
time: 398 us; the launch traced here: 396 us
  Pallas kernels  165 us (41%)
  waiting for transfers between devices  97 us (24%)
  blocking collectives  75.9 us (19%)
  local copies, waits for them, and re-layouts  21.8 us (5%)
  other arithmetic  18.7 us (5%)
  between operations  13.4 us (3%)
  starting transfers between devices  4.59 us (1%)
    pallas_call x2, Pallas kernels, channelize(): pl.pallas_call(lambda *refs: channelize_body(later, *refs), grid=(chunks...  124 us
    all_gather x1, waiting for transfers between devices, shards(): everything = lax.all_gather(merged[None], ('tm', 'stn'), axis=0, tiled=True)  97 us
    all_to_all x1, blocking collectives, shards(): lax.all_to_all(spectra, 'chan', split_axis=1, concat_axis=1, tiled=True)  75.9 us
    pallas_call x1, Pallas kernels, correlate_all(): pl.pallas_call(lambda *refs: correlate_body(scale, *refs), grid=(owned //...  40.3 us
  transfers between devices with their start and end apart: 2, of which 1 were waited for; matrix products, arithmetic and copies ran while one was open for 0% of the time, Pallas kernels for 16%

profile of v1, /device:TPU:0, one launch (start us, length us, event | category | flops | bytes accessed | tf_op | source)
XLA Modules:
  0.0 396.4 jit_solution(11469390940742127115)
XLA Ops:
  6.5 0.0 all-gather.2.cloned.1.call-start
  6.5 1.5 fusion.12
  8.0 3.9 multiply_convert_fusion
  11.9 3.2 copy.17
  15.1 4.6 %copy.16 = bf16[1,384,4096]{2,1,0:T(8,128)(2,1)} copy(bf16[1,384,4096]{1,2,0:T(8,128)(2,1)} %bitcast.10) | data formatting | bytes 6291456 | tf_op jit(solution)/shard_map/convert_element_type | solution.py:121
  19.7 0.0 copy-start
  19.7 0.7 neg.10
  20.4 1.2 copy-done
  21.6 1.1 maximum_bitcast_fusion
  22.7 5.2 %pad_maximum_fusion.refs_2_ = bf16[2,2,384,4096]{3,2,1,0:T(8,128)(2,1)} fusion(bf16[1,2,384,4096]{3,2,1,0:T(8,128)(2,1)S(1)} %get-tuple-element.6, bf16[1,2,384,4096]{3,2,1,0:T(8,128)(2,1)S(1)} %get-tuple-element.5), kind=kLoop, calls=%fused_computation | loop fusion | flops 6291456 | bytes 25165824 | tf_op jit(solution)/shard_map/stack | solution.py:123
  28.0 0.0 copy-start.1
  28.0 62.6 %shard_map.47 = f32[2,384,1536]{2,1,0:T(8,128)} custom-call(bf16[2,16,96,4096]{3,2,1,0:T(8,128)(2,1)} %refs_0_.3, f32[16,4096]{1,0:T(8,128)} %refs_1_.3, bf16[2,2,384,4096]{3,2,1,0:T(8,128)(2,1)} %pad_maximum_fusion.refs_2_), custom_call_target="tpu_custom_call" | custom-call | flops 38654705664 | bytes 60000000 | tf_op jit(solution)/shard_map/pallas_call | solution.py:194
  90.6 4.6 %collective-permute-start = (f32[2,384,1536]{2,1,0:T(8,128)}, f32[2,384,1536]{2,1,0:T(8,128)}, u32[]{:S(2)}, u32[]{:S(2)}) collective-permute-start(f32[2,384,1536]{2,1,0:T(8,128)} %shard_map.47), channel_id=1, source_target_pairs={{0,8},{8,16},{16,24},{1,9},{9,17},{17,25},{2,10},{10,18},{18,26},{... | collective-permute-start | bytes 14155784 | tf_op jit(solution)/shard_map/ppermute | solution.py:18
  95.2 0.0 copy-done.1
  95.2 0.1 mul.161
  95.3 61.8 %shard_map.46 = f32[2,384,1536]{2,1,0:T(8,128)} custom-call(bf16[2,16,96,4096]{3,2,1,0:T(8,128)(2,1)} %refs_0_.3, f32[16,4096]{1,0:T(8,128)} %refs_1_.3, bf16[2,2,384,4096]{3,2,1,0:T(8,128)(2,1)} %pad_maximum_fusion.refs_2_), custom_call_target="tpu_custom_call" | custom-call | flops 38654705664 | bytes 60000000 | tf_op jit(solution)/shard_map/pallas_call | solution.py:194
  157.1 0.0 collective-permute-done
  157.1 6.3 %multiply_convert_fusion.2 = bf16[2,384,1536]{2,1,0:T(8,128)(2,1)} fusion(f32[2,384,1536]{2,1,0:T(8,128)} %shard_map.46, f32[2,384,1536]{2,1,0:T(8,128)} %collective-permute-done, f32[1536]{0:T(1024)S(1)} %mul.161), kind=kLoop, calls=%fused_computation.5 | loop fusion | flops 3538944 | bytes 11802624 | tf_op jit(solution)/shard_map/convert_element_type | solution.py:283
  163.5 4.9 %reshape.199 = bf16[2,4,96,16,96]{4,3,2,1,0:T(8,128)(2,1)S(1)} reshape(bf16[2,384,1536]{2,1,0:T(8,128)(2,1)} %multiply_convert_fusion.2) | data formatting | bytes 4718592 | tf_op jit(solution)/shard_map/reshape | solution.py:285
  168.4 0.5 copy.20
  168.9 75.9 %all_to_all.5 = bf16[2,4,96,16,96]{4,3,2,0,1:T(8,128)(2,1)S(1)} all-to-all(bf16[2,4,96,16,96]{4,3,2,0,1:T(8,128)(2,1)S(1)} %copy.20), channel_id=1, replica_groups=mesh['tm'=4,'chan'=4,'stn'=2] {'chan'}, dimensions={1} | all-to-all | bytes 4718592 | tf_op jit(solution)/shard_map/all_to_all | solution.py:286
  244.8 4.0 %copy.21 = bf16[2,96,16,4,96]{4,3,2,1,0:T(4,128)(2,1)S(1)} copy(bf16[2,96,16,4,96]{4,2,1,0,3:T(8,128)(2,1)S(1)} %bitcast.12) | data formatting | bytes 4718592 | tf_op jit(solution)/shard_map/transpose | solution.py:287
  248.9 3.2 broadcast_in_dim_reshape.3
  252.1 0.0 all-gather.2.cloned.1.call-update
  252.1 97.0 %all-gather.2.cloned.1.call-done = bf16[8,2,96,16,384]{4,3,2,1,0:T(8,128)(2,1)} async-done(((bf16[1,2,96,16,384]{4,3,2,1,0:T(8,128)(2,1)}), bf16[8,2,96,16,384]{4,3,2,1,0:T(8,128)(2,1)}) %all-gather.2.cloned.1.call-update) | async-done | bytes 18874384 | tf_op jit(solution)/shard_map/all_gather | solution.py:288
  349.2 40.3 %shard_map.48 = f32[2,96,96,768]{3,2,1,0:T(8,128)} custom-call(s32[1]{0:T(128)} %bitcast.refs_0_, bf16[4,2,2,96,16,384]{5,4,3,2,1,0:T(8,128)(2,1)} %bitcast.9), custom_call_target="tpu_custom_call" | custom-call | tf_op jit(solution)/shard_map/pallas_call | solution.py:247
  (3 shorter events, 0.0 us)
Async XLA Ops:
  6.5 342.6 %all-gather.2.cloned.1.call-start = ((), (), s32[]{:S(2)}) async-start(), calls=%async_computation.1 | async-start | bytes 21233664 | tf_op jit(solution)/shard_map/all_gather | solution.py:288
  19.7 1.9 copy-start
  28.0 67.2 %copy-start.1 = (s32[96]{0:T(128)S(1)}, s32[96]{0:T(128)}, u32[]{:S(2)}) copy-start(s32[96]{0:T(128)} %param.7) | copy-start | bytes 1156
  90.6 66.5 %collective-permute-start = (f32[2,384,1536]{2,1,0:T(8,128)}, f32[2,384,1536]{2,1,0:T(8,128)}, u32[]{:S(2)}, u32[]{:S(2)}) collective-permute-start(f32[2,384,1536]{2,1,0:T(8,128)} %shard_map.47), channel_id=1, source_target_pairs={{0,8},{8,16},{16,24},{1,9},{9,17},{17,25},{2,10},{10,18},{18,26},{... | collective-permute-start | bytes 14155784 | tf_op jit(solution)/shard_map/ppermute | solution.py:18
Sparse Core Ops, SparseCore 0:
  252.3 96.8 all-gather.1

commit v2 on v1

--- a/solution.py
+++ b/solution.py
@@ -240,23 +240,32 @@
             out_ref[h, k] = product * scale
 
 
-def correlate_all(everything, which, inputs, scale):
-    n_time, n_station, _, owned, frames, width = everything.shape
+def correlate_part(everything, which, inputs, scale, owned, first, into):
+    n_time, n_station, _, held, frames, width = everything.shape
     count = 4
+    start = first // count
+    more = [] if into is None else [into]
     total = n_station * width
     return pl.pallas_call(
-        lambda *refs: correlate_body(scale, *refs),
-        grid=(owned // count,),
+        lambda *refs: correlate_body(scale, refs[0], refs[1], refs[-1]),
+        grid=(held // count,),
         in_specs=[
             pl.BlockSpec(memory_space=pltpu.SMEM),
             pl.BlockSpec(
                 (n_time, n_station, 2, count, frames, width), lambda j: (0, 0, 0, j, 0, 0)
             ),
-        ],
-        out_specs=pl.BlockSpec((2, count, inputs, total), lambda j: (0, j, 0, 0)),
+        ]
+        + [pl.BlockSpec(memory_space=pl.ANY) for _ in more],
+        out_specs=pl.BlockSpec((2, count, inputs, total), lambda j: (0, j + start, 0, 0)),
         out_shape=jax.ShapeDtypeStruct((2, owned, inputs, total), jnp.float32),
         compiler_params=pltpu.CompilerParams(vmem_limit_bytes=48 * 1024 * 1024),
-    )(which, everything)
+        input_output_aliases={2: 0} if more else {},
+        cost_estimate=pl.CostEstimate(
+            flops=500 * held * inputs * total,
+            bytes_accessed=8 * held * inputs * total,
+            transcendentals=0,
+        ),
+    )(which, everything, *more)
 
 
 def shards(voltages, coefficients, kept_channels, station_flags):
@@ -271,7 +280,7 @@
         and frames * GROUP % LANES == 0
         and n_chan * n_station == n_time * n_station
         and n_chan * inputs % LANES == 0
-        and channels // n_chan % 4 == 0
+        and channels // n_chan % 8 == 0
     )
     if not fits:
         return plain_shards(voltages, coefficients, kept_channels, station_flags)
@@ -283,13 +292,18 @@
     spectra = ((own + earlier) * weights).astype(jnp.bfloat16)
     owned = channels // n_chan
     spectra = spectra.reshape(2, n_chan, owned, frames, inputs)
-    turned = lax.all_to_all(spectra, "chan", split_axis=1, concat_axis=1, tiled=True)
-    merged = jnp.transpose(turned, (0, 2, 3, 1, 4)).reshape(2, owned, frames, n_chan * inputs)
-    everything = lax.all_gather(merged[None], ("tm", "stn"), axis=0, tiled=True)
-    everything = everything.reshape(n_time, n_station, *merged.shape)
-    which = lax.axis_index("tm") * n_station + lax.axis_index("stn")
+    which = (lax.axis_index("tm") * n_station + lax.axis_index("stn")).astype(jnp.int32)[None]
     scale = 1.0 / (frames * n_time)
-    return correlate_all(everything, which.astype(jnp.int32)[None], inputs, scale)
+    half = owned // 2
+    gathered = []
+    for first in (0, half):
+        sent = spectra[:, :, first : first + half]
+        turned = lax.all_to_all(sent, "chan", split_axis=1, concat_axis=1, tiled=True)
+        merged = jnp.transpose(turned, (0, 2, 3, 1, 4)).reshape(2, half, frames, n_chan * inputs)
+        everything = lax.all_gather(merged[None], ("tm", "stn"), axis=0, tiled=True)
+        gathered.append(everything.reshape(n_time, n_station, *merged.shape))
+    result = correlate_part(gathered[0], which, inputs, scale, owned, 0, None)
+    return correlate_part(gathered[1], which, inputs, scale, owned, half, result)
 
 
 def solution(mesh):

time: 398 us -> 364 us (0.915)
  waiting for transfers between devices: 97 us -> 53.2 us
  blocking collectives: 75.9 us -> 81.4 us
    all_gather x1 -> x2, waiting for transfers between devices: 97 us -> 53.2 us  [shards(): everything = lax.all_gather(merged[None], ('tm', 'stn'), axis=0, tiled=True)]
    all_to_all x1 -> x2, blocking collectives: 75.9 us -> 81.4 us  [shards(): lax.all_to_all(sent, 'chan', split_axis=1, concat_axis=1, tiled=True)]
    pallas_call x1 -> x2, Pallas kernels: 40.3 us -> 42.9 us  [correlate_part(): pl.pallas_call(lambda *refs: correlate_body(scale, refs[0], refs[1], refs...]
  transfers between devices with their start and end apart: 2 -> 3, of which waited for: 1 -> 2; matrix products, arithmetic and copies ran while one was open for 0% -> 1% of each run, Pallas kernels for 16% -> 23%
where the time goes in v2:
time: 364 us; the launch traced here: 363 us
  Pallas kernels  167 us (46%)
  blocking collectives  81.4 us (22%)
  waiting for transfers between devices  53.2 us (15%)
  local copies, waits for them, and re-layouts  24.1 us (7%)
  other arithmetic  18.7 us (5%)
  between operations  13.5 us (4%)
  starting transfers between devices  4.63 us (1%)
    pallas_call x2, Pallas kernels, channelize(): pl.pallas_call(lambda *refs: channelize_body(later, *refs), grid=(chunks...  124 us
    all_to_all x2, blocking collectives, shards(): lax.all_to_all(sent, 'chan', split_axis=1, concat_axis=1, tiled=True)  81.4 us
    all_gather x2, waiting for transfers between devices, shards(): everything = lax.all_gather(merged[None], ('tm', 'stn'), axis=0, tiled=True)  53.2 us
    pallas_call x2, Pallas kernels, correlate_part(): pl.pallas_call(lambda *refs: correlate_body(scale, refs[0], refs[1], refs...  42.9 us
  transfers between devices with their start and end apart: 3, of which 2 were waited for; matrix products, arithmetic and copies ran while one was open for 1% of the time, Pallas kernels for 23%

profile of v2, /device:TPU:0, one launch (start us, length us, event | category | flops | bytes accessed | tf_op | source)
XLA Modules:
  0.0 362.8 jit_solution(17318169656482330710)
XLA Ops:
  6.5 0.0 all-gather.5.cloned.1.call-start
  6.5 1.5 fusion.12
  8.0 3.9 %multiply_convert_fusion = (bf16[384,64,64]{0,2,1:T(8,128)(2,1)}, bf16[384,64,64]{0,2,1:T(8,128)(2,1)}) fusion(f32[384,64]{0,1:T(8,128)S(1)} %get-tuple-element.13, f32[384,64]{0,1:T(8,128)S(1)} %get-tuple-element.12, f32[384,64]{0,1:T(8,128)S(1)} %get-tuple-element.14, f32[384,64]{0,1:T(8,128)S(1)} %get-tuple-element.11), kind=kLoop, calls=%fused_computation.3 | loop fusion | flops 15728640 | bytes 6684672 | tf_op jit(solution)/shard_map/convert_element_type | solution.py:122
  11.9 3.2 copy.21
  15.1 4.6 %copy.20 = bf16[1,384,4096]{2,1,0:T(8,128)(2,1)} copy(bf16[1,384,4096]{1,2,0:T(8,128)(2,1)} %bitcast.11) | data formatting | bytes 6291456 | tf_op jit(solution)/shard_map/convert_element_type | solution.py:121
  19.7 0.0 copy-start
  19.7 0.7 neg.10
  20.4 1.2 copy-done
  21.6 1.1 maximum_bitcast_fusion
  22.7 5.2 %pad_maximum_fusion.refs_2_ = bf16[2,2,384,4096]{3,2,1,0:T(8,128)(2,1)} fusion(bf16[1,2,384,4096]{3,2,1,0:T(8,128)(2,1)S(1)} %get-tuple-element.8, bf16[1,2,384,4096]{3,2,1,0:T(8,128)(2,1)S(1)} %get-tuple-element.7), kind=kLoop, calls=%fused_computation | loop fusion | flops 6291456 | bytes 25165824 | tf_op jit(solution)/shard_map/stack | solution.py:123
  28.0 0.0 copy-start.2
  28.0 62.6 %shard_map.47 = f32[2,384,1536]{2,1,0:T(8,128)} custom-call(bf16[2,16,96,4096]{3,2,1,0:T(8,128)(2,1)} %refs_0_.3, f32[16,4096]{1,0:T(8,128)} %refs_1_.3, bf16[2,2,384,4096]{3,2,1,0:T(8,128)(2,1)} %pad_maximum_fusion.refs_2_), custom_call_target="tpu_custom_call" | custom-call | flops 38654705664 | bytes 60000000 | tf_op jit(solution)/shard_map/pallas_call | solution.py:194
  90.6 4.6 %collective-permute-start = (f32[2,384,1536]{2,1,0:T(8,128)}, f32[2,384,1536]{2,1,0:T(8,128)}, u32[]{:S(2)}, u32[]{:S(2)}) collective-permute-start(f32[2,384,1536]{2,1,0:T(8,128)} %shard_map.47), channel_id=1, source_target_pairs={{0,8},{8,16},{16,24},{1,9},{9,17},{17,25},{2,10},{10,18},{18,26},{... | collective-permute-start | bytes 14155784 | tf_op jit(solution)/shard_map/ppermute | solution.py:18
  95.2 0.0 copy-done.2
  95.2 0.1 mul.161
  95.3 61.8 %shard_map.46 = f32[2,384,1536]{2,1,0:T(8,128)} custom-call(bf16[2,16,96,4096]{3,2,1,0:T(8,128)(2,1)} %refs_0_.3, f32[16,4096]{1,0:T(8,128)} %refs_1_.3, bf16[2,2,384,4096]{3,2,1,0:T(8,128)(2,1)} %pad_maximum_fusion.refs_2_), custom_call_target="tpu_custom_call" | custom-call | flops 38654705664 | bytes 60000000 | tf_op jit(solution)/shard_map/pallas_call | solution.py:194
  157.1 0.0 collective-permute-done
  157.1 6.3 %multiply_convert_fusion.2 = bf16[2,384,1536]{2,1,0:T(8,128)(2,1)} fusion(f32[2,384,1536]{2,1,0:T(8,128)} %shard_map.46, f32[2,384,1536]{2,1,0:T(8,128)} %collective-permute-done, f32[1536]{0:T(1024)S(1)} %mul.161), kind=kLoop, calls=%fused_computation.5 | loop fusion | flops 3538944 | bytes 11802624 | tf_op jit(solution)/shard_map/convert_element_type | solution.py:292
  163.5 4.9 %reshape.202 = bf16[2,4,96,16,96]{4,3,2,1,0:T(8,128)(2,1)S(1)} reshape(bf16[2,384,1536]{2,1,0:T(8,128)(2,1)} %multiply_convert_fusion.2) | data formatting | bytes 4718592 | tf_op jit(solution)/shard_map/reshape | solution.py:294
  168.4 1.7 fusion.13
  170.0 0.3 copy.29
  170.3 0.0 copy-start.1
  170.3 42.4 %all_to_all.10 = bf16[2,4,48,16,96]{4,3,2,0,1:T(8,128)(2,1)S(1)} all-to-all(bf16[2,4,48,16,96]{4,3,2,0,1:T(8,128)(2,1)S(1)} %copy.29), channel_id=1, replica_groups=mesh['tm'=4,'chan'=4,'stn'=2] {'chan'}, dimensions={1} | all-to-all | bytes 2359296 | tf_op jit(solution)/shard_map/all_to_all | solution.py:301
  212.7 2.0 copy.27
  214.7 1.9 broadcast_in_dim_reshape.7
  216.6 0.0 all-gather.5.cloned.1.call-update
  216.6 0.0 all-gather.3.cloned.1.call-start
  216.7 0.0 copy-done.1
  216.7 0.3 copy.28
  217.0 39.0 %all_to_all.11 = bf16[2,4,48,16,96]{4,3,2,0,1:T(8,128)(2,1)S(1)} all-to-all(bf16[2,4,48,16,96]{4,3,2,0,1:T(8,128)(2,1)S(1)} %copy.28), channel_id=1, replica_groups=mesh['tm'=4,'chan'=4,'stn'=2] {'chan'}, dimensions={1} | all-to-all | bytes 2359296 | tf_op jit(solution)/shard_map/all_to_all | solution.py:301
  256.0 2.0 copy.25
  258.0 1.9 broadcast_in_dim_reshape.6
  259.9 0.0 all-gather.3.cloned.1.call-update
  259.9 13.8 %all-gather.5.cloned.1.call-done = bf16[8,2,48,16,384]{4,3,2,1,0:T(8,128)(2,1)} async-done(((bf16[1,2,48,16,384]{4,3,2,1,0:T(8,128)(2,1)}), bf16[8,2,48,16,384]{4,3,2,1,0:T(8,128)(2,1)}) %all-gather.5.cloned.1.call-update) | async-done | bytes 9437200 | tf_op jit(solution)/shard_map/all_gather | solution.py:303
  273.8 21.4 %shard_map.48.refs_2_ = f32[2,96,96,768]{3,2,1,0:T(8,128)} custom-call(s32[1]{0:T(128)} %bitcast.refs_0_, bf16[4,2,2,48,16,384]{5,4,3,2,1,0:T(8,128)(2,1)} %bitcast.13), custom_call_target="tpu_custom_call" | custom-call | flops 1769472000 | bytes 28311552 | tf_op jit(solution)/shard_map/pallas_call | solution.py:249
  295.2 39.3 %all-gather.3.cloned.1.call-done = bf16[8,2,48,16,384]{4,3,2,1,0:T(8,128)(2,1)} async-done(((bf16[1,2,48,16,384]{4,3,2,1,0:T(8,128)(2,1)}), bf16[8,2,48,16,384]{4,3,2,1,0:T(8,128)(2,1)}) %all-gather.3.cloned.1.call-update) | async-done | bytes 9437200 | tf_op jit(solution)/shard_map/all_gather | solution.py:303
  334.5 21.5 %shard_map.49 = f32[2,96,96,768]{3,2,1,0:T(8,128)} custom-call(s32[1]{0:T(128)} %bitcast.refs_0_, bf16[4,2,2,48,16,384]{5,4,3,2,1,0:T(8,128)(2,1)} %bitcast.14, f32[2,96,96,768]{3,2,1,0:T(8,128)} %shard_map.48.refs_2_), custom_call_target="tpu_custom_call", output_to_operand_aliasing={{}: (2, {})} | custom-call | flops 1769472000 | bytes 28311552 | tf_op jit(solution)/shard_map/pallas_call | solution.py:249
  (3 shorter events, 0.0 us)
Async XLA Ops:
  6.5 267.2 %all-gather.5.cloned.1.call-start = ((), (), s32[]{:S(2)}) async-start(), calls=%async_computation.3 | async-start | bytes 10616832 | tf_op jit(solution)/shard_map/all_gather | solution.py:303
  19.7 1.9 copy-start
  28.0 67.2 %copy-start.2 = (s32[96]{0:T(128)S(1)}, s32[96]{0:T(128)}, u32[]{:S(2)}) copy-start(s32[96]{0:T(128)} %param.7) | copy-start | bytes 1156
  90.6 66.5 %collective-permute-start = (f32[2,384,1536]{2,1,0:T(8,128)}, f32[2,384,1536]{2,1,0:T(8,128)}, u32[]{:S(2)}, u32[]{:S(2)}) collective-permute-start(f32[2,384,1536]{2,1,0:T(8,128)} %shard_map.47), channel_id=1, source_target_pairs={{0,8},{8,16},{16,24},{1,9},{9,17},{17,25},{2,10},{10,18},{18,26},{... | collective-permute-start | bytes 14155784 | tf_op jit(solution)/shard_map/ppermute | solution.py:18
  170.3 46.3 %copy-start.1 = (bf16[2,4,48,16,96]{4,3,2,1,0:T(8,128)(2,1)S(1)}, bf16[2,4,48,16,96]{4,3,2,1,0:T(8,128)(2,1)}, u32[]{:S(2)}) copy-start(bf16[2,4,48,16,96]{4,3,2,1,0:T(8,128)(2,1)} %get-tuple-element.6) | copy-start | bytes 3538948
  216.6 117.9 %all-gather.3.cloned.1.call-start = ((), (), s32[]{:S(2)}) async-start(), calls=%async_computation.2 | async-start | bytes 10616832 | tf_op jit(solution)/shard_map/all_gather | solution.py:303
Sparse Core Ops, SparseCore 0:
  216.7 56.9 all-gather.4
  275.6 58.8 all-gather.2
